TPU v7x, 32 devices: a whole 2x2x4 slice. The times are simulated.
32 devices in a mesh: group: 2 (over y), ep: 4 (over z), tp: 4 (over x, core).
Axes of the slice: x: 2, y: 2, z: 4, core: 2. Of those that a mesh axis runs over, the one named last changes fastest.
Arguments:
- tokens: bfloat16 [512, 3584], P(('group', 'ep'), 'tp'), parts along dimension 0, may hold values from -6 to 6
- routes: int32 [512, 2], P(('group', 'ep')), parts along dimension 0, may hold values from 0 to 3, all different within a row; in each aligned block of 64 rows (0 to 63, 64 to 127, ...) at most 64 rows name the same one
- scores: float32 [512, 2], P(('group', 'ep')), parts along dimension 0, may hold values from 0.05 to 1
- w_up: bfloat16 [4, 3584, 1024], P('ep', 'tp'), may hold values from -0.09375 to 0.09375
- w_down: bfloat16 [4, 1024, 3584], P('ep', None, 'tp'), may hold values from -0.1875 to 0.1875
Outputs:
- mixed: bfloat16 [512, 3584], P(('group', 'ep'), 'tp'), parts along dimension 0
There are 2 independent parts, one for each index of `group`. A program takes and returns all parts, laid end to end along the dimension named above; an argument that names none is the same for every part. Nothing has to cross between parts.
Inputs may be any that keep to these rules, and one draw needn't show every extreme that they name: `routes`: within the rows of one index of ep, each expert is named at most 64 times, and no row names an expert twice.
All inputs are finite; a program needn't handle non-finite values.
Results may differ from a plain program's by a relative error of at most 0.015.
Values may be sent and summed in bfloat16 or wider, within the bound.
A program may use at most 64 MiB of HBM per device.

v0:
```python
import jax
import jax.numpy as jnp
from jax import lax
from jax.sharding import PartitionSpec as P

SCALE = 2.5


def body(tokens, routes, scores, w_up, w_down):
    rows_here, quarter = tokens.shape
    chosen = routes.shape[1]
    owners = lax.axis_size("ep")
    capacity = 2 * rows_here * chosen // owners
    flat_ids = routes.reshape(-1)
    onehot = (flat_ids[:, None] == jnp.arange(owners, dtype=jnp.int32)[None, :]).astype(jnp.int32)
    slot_rank = jnp.sum((jnp.cumsum(onehot, axis=0) - onehot) * onehot, axis=1)
    target = flat_ids * capacity + slot_rank
    pair_token = jnp.arange(rows_here * chosen, dtype=jnp.int32) // chosen
    matches = target[None, :] == jnp.arange(owners * capacity, dtype=jnp.int32)[:, None]
    source = jnp.sum(jnp.where(matches, pair_token[None, :] + 1, 0), axis=1) - 1
    picked = jnp.take(tokens, jnp.maximum(source, 0), axis=0)
    outgoing = jnp.where((source >= 0)[:, None], picked, jnp.zeros_like(picked)).reshape(
        owners, capacity, quarter
    )
    up_local = w_up[0]
    down_local = w_down[0]
    arrived = lax.all_to_all(outgoing, "ep", split_axis=0, concat_axis=0, tiled=True)
    senders, slot_count, columns = arrived.shape
    flat_rows = arrived.reshape(senders * slot_count, columns)
    partial_value = jnp.dot(flat_rows, up_local, preferred_element_type=jnp.float32)
    hidden = jax.nn.silu(
        lax.psum(partial_value.astype(jnp.bfloat16), "tp").astype(jnp.float32)
    ).astype(jnp.bfloat16)
    result = jnp.dot(hidden, down_local, preferred_element_type=jnp.float32).astype(jnp.bfloat16)
    returned_rows = lax.all_to_all(
        result.reshape(senders, slot_count, columns), "ep", split_axis=0, concat_axis=0, tiled=True
    )
    back_flat = returned_rows.reshape(owners * capacity, quarter)
    gathered = (
        jnp.take(back_flat, target, axis=0).reshape(rows_here, chosen, quarter).astype(jnp.float32)
    )
    weights = SCALE * scores / jnp.sum(scores, axis=1, keepdims=True)
    mixed = jnp.einsum("tk,tkd->td", weights, gathered, precision=lax.Precision.HIGHEST)
    return mixed.astype(jnp.bfloat16)


def solution(mesh):
    in_specs = (
        P(("group", "ep"), "tp"),
        P(("group", "ep"), None),
        P(("group", "ep"), None),
        P("ep", "tp", None),
        P("ep", None, "tp"),
    )
    out_specs = P(("group", "ep"), "tp")
    return jax.shard_map(body, mesh=mesh, in_specs=in_specs, out_specs=out_specs, check_vma=False)
```

profile of v0, /device:TPU:0, one launch (start us, length us, event | category | flops | bytes accessed | tf_op | source)
XLA Modules:
  0.0 92.5 jit_solution(10596354337231958427)
XLA Ops:
  6.5 0.0 copy-start
  6.5 0.0 copy-start.1
  6.5 0.0 all-reduce.2.cloned.1.call-start
  6.5 0.9 copy.12
  7.5 0.1 reshape.122
  7.6 0.1 fusion.18
  7.7 0.2 reduce_window_sum.11
  7.9 0.2 select_reduce_fusion.1
  8.1 0.1 select_reduce_fusion
  8.2 0.1 ge.29
  8.3 0.1 le.31
  8.4 0.0 copy-done.1
  8.4 1.2 %gather_fusion = bf16[256,896]{1,0:T(8,128)(2,1)S(1)} fusion(bf16[64,896]{1,0:T(8,128)(2,1)S(1)} %copy-done.1, s32[1024]{0:T(1024)S(1)} %pad_clamp_fusion.1), kind=kCustom, calls=%fused_computation | custom fusion | bytes 918528 | tf_op jit(solution)/shard_map/jit(_take)/gather | solution.py:21
  9.6 0.2 select_select_fusion
  9.8 19.2 %all_to_all.10 = bf16[4,64,896]{2,1,0:T(8,128)(2,1)S(1)} all-to-all(bf16[4,64,896]{2,1,0:T(8,128)(2,1)S(1)} %select_select_fusion), channel_id=1, replica_groups=mesh['group'=2,'ep'=4,'tp'=4] {'ep'}, dimensions={0} | all-to-all | bytes 917504 | tf_op jit(solution)/shard_map/all_to_all | solution.py:27
  29.0 0.0 copy-start.2
  29.0 0.0 copy-done
  29.0 1.6 %fusion.4 = bf16[256,1024]{1,0:T(8,128)(2,1)} fusion(bf16[256,896]{1,0:T(8,128)(2,1)S(1)} %bitcast.29, bf16[1,896,1024]{2,1,0:T(8,128)(2,1)S(1)} %copy-done), kind=kOutput, calls=%fused_computation.8 | convolution fusion | flops 470024192 | bytes 2818048 | tf_op jit(solution)/shard_map/dot_general | solution.py:30
  30.5 0.0 all-reduce.2.cloned.1.call-update
  30.5 0.1 reduce_sum.33
  30.7 0.0 copy-done.2
  30.7 0.1 copy.15
  30.8 0.1 mul.48
  30.9 0.1 copy.13
  31.0 0.0 copy-start.3
  31.0 32.0 %all-reduce.2.cloned.1.call-done = bf16[256,1024]{1,0:T(8,128)(2,1)} async-done(((bf16[256,1024]{1,0:T(8,128)(2,1)}), bf16[256,1024]{1,0:T(8,128)(2,1)}) %all-reduce.2.cloned.1.call-update) | async-done | bytes 524304 | tf_op jit(solution)/shard_map/psum | solution.py:32
  63.0 3.2 %fusion.7 = bf16[256,896]{1,0:T(8,128)(2,1)} fusion(bf16[1,1024,896]{2,1,0:T(8,128)(2,1)} %param.9, bf16[256,1024]{1,0:T(8,128)(2,1)} %all-reduce.2.cloned.1.call-done), kind=kOutput, calls=%fused_computation.9 | convolution fusion | flops 471564288 | bytes 2818048 | tf_op jit(solution)/shard_map/dot_general | solution.py:34
  66.2 4.6 %all-to-all-start.1 = ((bf16[4,64,896]{2,1,0:T(8,128)(2,1)}), bf16[4,64,896]{2,1,0:T(8,128)(2,1)S(1)}, u32[]{:S(2)}, u32[]{:S(2)}) async-start(bf16[4,64,896]{2,1,0:T(8,128)(2,1)} %bitcast.5), calls=%async_computation.1 | async-start | bytes 917504 | tf_op jit(solution)/shard_map/all_to_all | solution.py:35
  70.8 0.1 copy.14
  70.9 0.0 copy-done.3
  71.0 0.1 copy.16
  71.1 11.9 %all-to-all-done.1 = bf16[4,64,896]{2,1,0:T(8,128)(2,1)S(1)} async-done(((bf16[4,64,896]{2,1,0:T(8,128)(2,1)}), bf16[4,64,896]{2,1,0:T(8,128)(2,1)S(1)}, u32[]{:S(2)}, u32[]{:S(2)}) %all-to-all-start.1) | async-done | bytes 458784 | tf_op jit(solution)/shard_map/all_to_all | solution.py:35
  83.0 0.9 gather_fusion.1
  83.8 0.1 gather.15
  83.9 1.0 %fusion.16 = bf16[64,1,896]{2,1,0:T(2,128)(2,1)S(1)} fusion(f32[64,2,1]{1,2,0:T(1,128)S(1)} %copy.16, bf16[64,2,896]{2,1,0:T(2,128)(2,1)S(1)} %gather.15, pred[64,2]{1,0:T(8,128)(4,1)S(1)} %copy.14), kind=kOutput, calls=%fused_computation.18 | convolution fusion | flops 1490944 | bytes 344704 | tf_op jit(solution)/shard_map/tk,tkd->td/dot_general | solution.py:43
  85.0 0.7 copy.19
  (10 shorter events, 0.1 us)
Async XLA Ops:
  6.5 22.4 %copy-start = (bf16[1,896,1024]{2,1,0:T(8,128)(2,1)S(1)}, bf16[1,896,1024]{2,1,0:T(8,128)(2,1)}, u32[]{:S(2)}) copy-start(bf16[1,896,1024]{2,1,0:T(8,128)(2,1)} %param.8) | copy-start | bytes 5505028
  6.5 1.8 %copy-start.1 = (bf16[64,896]{1,0:T(8,128)(2,1)S(1)}, bf16[64,896]{1,0:T(8,128)(2,1)}, u32[]{:S(2)}) copy-start(bf16[64,896]{1,0:T(8,128)(2,1)} %param.5) | copy-start | bytes 344068
  6.5 56.5 %all-reduce.2.cloned.1.call-start = ((), (), s32[]{:S(2)}) async-start(), calls=%async_computation.2 | async-start | bytes 1048576 | tf_op jit(solution)/shard_map/psum | solution.py:32
  29.0 1.7 %copy-start.2 = (s32[64,2]{0,1:T(2,128)S(1)}, s32[64,2]{0,1:T(2,128)}, u32[]{:S(2)}) copy-start(s32[64,2]{0,1:T(2,128)} %param.6) | copy-start | bytes 1540
  31.0 39.9 %copy-start.3 = (f32[64,2]{0,1:T(2,128)S(1)}, f32[64,2]{0,1:T(2,128)}, u32[]{:S(2)}) copy-start(f32[64,2]{0,1:T(2,128)} %param.7) | copy-start | bytes 1540
  66.2 16.8 %all-to-all-start.1 = ((bf16[4,64,896]{2,1,0:T(8,128)(2,1)}), bf16[4,64,896]{2,1,0:T(8,128)(2,1)S(1)}, u32[]{:S(2)}, u32[]{:S(2)}) async-start(bf16[4,64,896]{2,1,0:T(8,128)(2,1)} %bitcast.5), calls=%async_computation.1 | async-start | bytes 917504 | tf_op jit(solution)/shard_map/all_to_all | solution.py:35
Sparse Core Ops, SparseCore 0:
  30.7 32.2 all-reduce.1
where the time goes:
time: 92.7 us; the launch traced here: 92.5 us
  waiting for transfers between devices  43.9 us (47%)
  blocking collectives  19.2 us (21%)
  between operations  13.5 us (15%)
  matrix products  5.79 us (6%)
  local copies, waits for them, and re-layouts  4.71 us (5%)
  starting transfers between devices  4.61 us (5%)
    psum x1, waiting for transfers between devices, body(): lax.psum(partial_value.astype(jnp.bfloat16), 'tp').astype(jnp.float32)  32 us
    all_to_all x1, blocking collectives, body(): lax.all_to_all(outgoing, 'ep', split_axis=0, concat_axis=0, tiled=True)  19.2 us
    all_to_all x1, waiting for transfers between devices, body(): lax.all_to_all(result.reshape(senders, slot_count, columns), 'ep', split_...  11.9 us
    all_to_all x1, starting transfers between devices, body(): lax.all_to_all(result.reshape(senders, slot_count, columns), 'ep', split_...  4.61 us
    dot_general x1, matrix products, body(): jnp.dot(hidden, down_local, preferred_element_type=jnp.float32)  3.2 us
  transfers between devices with their start and end apart: 2, of which 2 were waited for; matrix products, arithmetic and copies ran while one was open for 1% of the time, Pallas kernels for 0%

commit v1 on v0

--- a/solution.py
+++ b/solution.py
@@ -1,9 +1,176 @@
+import functools
+
 import jax
 import jax.numpy as jnp
 from jax import lax
+from jax.experimental import pallas as pl
+from jax.experimental.pallas import tpu as pltpu
 from jax.sharding import PartitionSpec as P
 
 SCALE = 2.5
+MESH = pl.DeviceIdType.MESH
+N = 4
+
+
+def partner(e, k):
+    return (e, e + 1 - 2 * lax.rem(e, 2), lax.rem(e + 2, N), N - 1 - e)[k]
+
+
+def kernel(
+    tok_hbm, routes_ref, scores_ref, up_hbm, down_hbm, out_ref,
+    up, down, arrived, part, from_core, from_chip, pair_sum, outgoing, hidden, result, returned,
+    load_sem, a_send, a_recv, core_send, core_recv, chip_send, chip_recv, hid_send, hid_recv, c_send, c_recv,
+):
+    e = lax.axis_index("ep")
+    tp = lax.axis_index("tp")
+    core = lax.rem(tp, 2)
+    other = 1 - core
+    sibling = {"tp": tp + 1 - 2 * core}
+    across = {"tp": lax.rem(tp + 2, N)}
+    rows = out_ref.shape[0]
+
+    load_tok = pltpu.make_async_copy(tok_hbm, arrived.at[0], load_sem.at[0])
+    load_up = pltpu.make_async_copy(up_hbm.at[0], up, load_sem.at[1])
+    load_down = pltpu.make_async_copy(down_hbm.at[0], down, load_sem.at[2])
+    load_tok.start()
+    load_up.start()
+    load_down.start()
+
+    barrier = pltpu.get_barrier_semaphore()
+    for k in range(1, N):
+        pl.semaphore_signal(barrier, inc=1, device_id={"ep": partner(e, k)}, device_id_type=MESH)
+    pl.semaphore_signal(barrier, inc=1, device_id=sibling, device_id_type=MESH)
+    pl.semaphore_signal(barrier, inc=1, device_id=across, device_id_type=MESH)
+    pl.semaphore_wait(barrier, N + 1)
+
+    def remote(src, dst, send, recv, k, device):
+        return pltpu.make_async_remote_copy(
+            src_ref=src, dst_ref=dst, send_sem=send.at[k], recv_sem=recv.at[k],
+            device_id=device, device_id_type=MESH,
+        )
+
+    def a_copy(k):
+        return remote(tok_hbm, arrived.at[k], a_send, a_recv, k, {"ep": partner(e, k)})
+
+    def core_copy(k):
+        return remote(part.at[k, other], from_core.at[k], core_send, core_recv, k, sibling)
+
+    def chip_copy(k):
+        return remote(outgoing.at[k], from_chip.at[k], chip_send, chip_recv, k, across)
+
+    def hid_copy(k):
+        return remote(hidden.at[k, core], hidden.at[k, core], hid_send, hid_recv, k, sibling)
+
+    def c_copy(k):
+        return remote(result.at[k], returned.at[k], c_send, c_recv, k, {"ep": partner(e, k)})
+
+    for k in range(1, N):
+        a_copy(k).start()
+
+    half = rows // 2
+
+    scores = scores_ref[...]
+    weights = SCALE * scores / jnp.sum(scores, axis=0, keepdims=True)
+    routes = routes_ref[...]
+    square = (rows, rows)
+    diagonal = lax.broadcasted_iota(jnp.int32, square, 0) == lax.broadcasted_iota(jnp.int32, square, 1)
+    factors = []
+    for k in range(N):
+        row = jnp.sum(jnp.where(routes == partner(e, k), weights, 0.0), axis=0, keepdims=True)
+        factors.append(jnp.sum(jnp.where(diagonal, row, 0.0), axis=1, keepdims=True))
+
+    def up_stage(k):
+        if k == 0:
+            load_tok.wait()
+            load_up.wait()
+        else:
+            a_copy(k).wait_recv()
+        value = jnp.dot(arrived[k], up[...], preferred_element_type=jnp.float32).astype(jnp.bfloat16)
+        part[k] = value.reshape(2, half, value.shape[1])
+        core_copy(k).start()
+
+    def chip_stage(k):
+        core_copy(k).wait_recv()
+        both = part[k, core].astype(jnp.float32) + from_core[k].astype(jnp.float32)
+        pair_sum[k] = both
+        outgoing[k] = both.astype(jnp.bfloat16)
+        chip_copy(k).start()
+
+    def hidden_stage(k):
+        chip_copy(k).wait_recv()
+        value = pair_sum[k] + from_chip[k].astype(jnp.float32)
+        hidden[k, core] = (value / (1.0 + jnp.exp(-value))).astype(jnp.bfloat16)
+        hid_copy(k).start()
+
+    def down_stage(k):
+        hid_copy(k).wait_recv()
+        if k == 0:
+            load_down.wait()
+        rows_in = hidden[k].reshape(rows, hidden.shape[3])
+        value = jnp.dot(rows_in, down[...], preferred_element_type=jnp.float32).astype(jnp.bfloat16)
+        if k == 0:
+            returned[0] = value
+        else:
+            result[k] = value
+            c_copy(k).start()
+
+    order = (0, 1, 3, 2)
+    for t in range(N + 3):
+        for lag, stage in ((3, down_stage), (2, hidden_stage), (1, chip_stage), (0, up_stage)):
+            if 0 <= t - lag < N:
+                stage(order[t - lag])
+
+    mixed = jnp.zeros(out_ref.shape, jnp.float32)
+    for k in order:
+        if k > 0:
+            c_copy(k).wait_recv()
+        mixed = mixed + factors[k] * returned[k].astype(jnp.float32)
+    out_ref[...] = mixed.astype(out_ref.dtype)
+
+    for k in range(N):
+        core_copy(k).wait_send()
+        chip_copy(k).wait_send()
+        hid_copy(k).wait_send()
+        if k > 0:
+            a_copy(k).wait_send()
+            c_copy(k).wait_send()
+
+
+def dense_body(tokens, routes, scores, w_up, w_down):
+    rows, quarter = tokens.shape
+    width = w_up.shape[2]
+    half = rows // 2
+    bf16, f32 = jnp.bfloat16, jnp.float32
+    vmem = pl.BlockSpec(memory_space=pltpu.VMEM)
+    anywhere = pl.BlockSpec(memory_space=pl.ANY)
+    dma = pltpu.SemaphoreType.DMA
+    return pl.pallas_call(
+        kernel,
+        out_shape=jax.ShapeDtypeStruct((rows, quarter), bf16),
+        in_specs=[anywhere, vmem, vmem, anywhere, anywhere],
+        out_specs=vmem,
+        scratch_shapes=[
+            pltpu.VMEM((quarter, width), bf16),
+            pltpu.VMEM((width, quarter), bf16),
+            pltpu.VMEM((N, rows, quarter), bf16),
+            pltpu.VMEM((N, 2, half, width), bf16),
+            pltpu.VMEM((N, half, width), bf16),
+            pltpu.VMEM((N, half, width), bf16),
+            pltpu.VMEM((N, half, width), f32),
+            pltpu.VMEM((N, half, width), bf16),
+            pltpu.VMEM((N, 2, half, width), bf16),
+            pltpu.VMEM((N, rows, quarter), bf16),
+            pltpu.VMEM((N, rows, quarter), bf16),
+            dma((3,)),
+        ] + [dma((N,))] * 10,
+        compiler_params=pltpu.CompilerParams(
+            collective_id=0, has_side_effects=True, vmem_limit_bytes=60 * 1024 * 1024
+        ),
+        cost_estimate=pl.CostEstimate(
+            flops=4 * N * rows * quarter * width, bytes_accessed=4 * quarter * width, transcendentals=N * rows * width
+        ),
+        name="expert_layer",
+    )(tokens, routes.T, scores.T, w_up, w_down)
 
 
 def body(tokens, routes, scores, w_up, w_down):
@@ -53,4 +220,6 @@
         P("ep", None, "tp"),
     )
     out_specs = P(("group", "ep"), "tp")
-    return jax.shard_map(body, mesh=mesh, in_specs=in_specs, out_specs=out_specs, check_vma=False)
+    shape = mesh.shape
+    small = shape["ep"] == N and shape["tp"] == N
+    return jax.shard_map(dense_body if small else body, mesh=mesh, in_specs=in_specs, out_specs=out_specs, check_vma=False)

time: 92.7 us -> 38.3 us (0.41)
  waiting for transfers between devices: 43.9 us -> 0 us
  Pallas kernels: 0 us -> 36.5 us
  blocking collectives: 19.2 us -> 0 us
  between operations: 13.5 us -> 0.01 us
  matrix products: 5.79 us -> 0 us
  starting transfers between devices: 4.61 us -> 0 us
  local copies, waits for them, and re-layouts: 4.71 us -> 1.55 us
    pallas_call x0 -> x1, Pallas kernels: none -> 36.5 us  [dense_body(): pl.pallas_call(kernel, out_shape=jax.ShapeDtypeStruct((rows, quarter), bf...]
    psum x1 -> x0, waiting for transfers between devices: 32 us -> none  [body(): lax.psum(partial_value.astype(jnp.bfloat16), 'tp').astype(jnp.float32)]
    all_to_all x1 -> x0, blocking collectives: 19.2 us -> none  [body(): lax.all_to_all(outgoing, 'ep', split_axis=0, concat_axis=0, tiled=True)]
    all_to_all x1 -> x0, waiting for transfers between devices: 11.9 us -> none  [body(): lax.all_to_all(result.reshape(senders, slot_count, columns), 'ep', split_...]
    dot_general x3 -> x0, matrix products: 5.79 us -> none  [the longest x1 3.2 us: body(): jnp.dot(hidden, down_local, preferred_element_type=jnp.float32)]
    all_to_all x1 -> x0, starting transfers between devices: 4.61 us -> none  [body(): lax.all_to_all(result.reshape(senders, slot_count, columns), 'ep', split_...]
    gather x3 -> x0, local copies, waits for them, and re-layouts: 2.17 us -> none  [the longest x1 1.2 us: body(): picked = jnp.take(tokens, jnp.maximum(source, 0), axis=0)]
  transfers between devices with their start and end apart: 2 -> 0, of which waited for: 2 -> 0; matrix products, arithmetic and copies ran while one was open for 1% -> 0% of each run, Pallas kernels for 0% -> 0%
where the time goes in v1:
time: 38.3 us; the launch traced here: 38.1 us
  Pallas kernels  36.5 us (95%)
  local copies, waits for them, and re-layouts  1.55 us (4%)
    pallas_call x1, Pallas kernels, dense_body(): pl.pallas_call(kernel, out_shape=jax.ShapeDtypeStruct((rows, quarter), bf...  36.5 us
    unnamed x1, local copies, waits for them, and re-layouts  1.55 us

profile of v1, /device:TPU:0, one launch (start us, length us, event | category | flops | bytes accessed | tf_op | source)
XLA Modules:
  0.0 38.1 jit_solution(534593658381642550)
XLA Ops:
  0.0 36.5 %expert_layer.1 = bf16[64,896]{1,0:T(8,128)(2,1)} custom-call(bf16[64,896]{1,0:T(8,128)(2,1)} %tok_hbm.1, s32[2,64]{1,0:T(2,128)} %bitcast.2, f32[2,64]{1,0:T(2,128)} %bitcast.3, bf16[1,896,1024]{2,1,0:T(8,128)(2,1)} %up_hbm.1, bf16[1,1024,896]{2,1,0:T(8,128)(2,1)} %down_hbm.1), custom_call_target="tpu_custom_call" | custom-call | flops 939524096 | bytes 3670016 | tf_op jit(solution)/shard_map/expert_layer/pallas_call | solution.py:147
  36.6 1.6 %copy.7 = bf16[64,896]{1,0:T(8,128)(2,1)} copy(bf16[64,896]{1,0:T(8,128)(2,1)} %expert_layer.1) | data formatting | bytes 229376

commit v2 on v1

--- a/solution.py
+++ b/solution.py
@@ -12,17 +12,33 @@
 N = 4
 
 
-def partner(e, k):
-    return (e, e + 1 - 2 * lax.rem(e, 2), lax.rem(e + 2, N), N - 1 - e)[k]
+SCHEDULE = (
+    "u0 c0 S2 u1 "
+    "F c1 S3 h0 "
+    "d0 u2 c2 u3 "
+    "c3 h1 d1 h2 "
+    "d2 h3 d3 "
+)
+
+
+def partners(e):
+    middle = lax.rem((e + 1) // 2, 2)
+    slots = (0, 1, 2 + middle, 3 - middle)
+    near = e + 1 - 2 * lax.rem(e, 2)
+    cross, flip = lax.rem(e + 2, N), N - 1 - e
+    second = middle * flip + (1 - middle) * cross
+    third = middle * cross + (1 - middle) * flip
+    return middle, slots, (e, near, second, third)
 
 
 def kernel(
     tok_hbm, routes_ref, scores_ref, up_hbm, down_hbm, out_ref,
     up, down, arrived, part, from_core, from_chip, pair_sum, outgoing, hidden, result, returned,
-    load_sem, a_send, a_recv, core_send, core_recv, chip_send, chip_recv, hid_send, hid_recv, c_send, c_recv,
+    load_sem, a_send, a_recv, core_send, core_recv, chip_send, chip_recv, hid_send, hid_recv, c_send, c_recv, far_sem,
 ):
     e = lax.axis_index("ep")
     tp = lax.axis_index("tp")
+    middle, slots, peers = partners(e)
     core = lax.rem(tp, 2)
     other = 1 - core
     sibling = {"tp": tp + 1 - 2 * core}
@@ -37,11 +53,15 @@
     load_down.start()
 
     barrier = pltpu.get_barrier_semaphore()
-    for k in range(1, N):
-        pl.semaphore_signal(barrier, inc=1, device_id={"ep": partner(e, k)}, device_id_type=MESH)
+    pl.semaphore_signal(barrier, inc=1, device_id={"ep": peers[1]}, device_id_type=MESH)
+
+    @pl.when(middle == 1)
+    def _():
+        pl.semaphore_signal(barrier, inc=1, device_id={"ep": peers[2]}, device_id_type=MESH)
+
     pl.semaphore_signal(barrier, inc=1, device_id=sibling, device_id_type=MESH)
     pl.semaphore_signal(barrier, inc=1, device_id=across, device_id_type=MESH)
-    pl.semaphore_wait(barrier, N + 1)
+    pl.semaphore_wait(barrier, 3 + middle)
 
     def remote(src, dst, send, recv, k, device):
         return pltpu.make_async_remote_copy(
@@ -50,7 +70,10 @@
         )
 
     def a_copy(k):
-        return remote(tok_hbm, arrived.at[k], a_send, a_recv, k, {"ep": partner(e, k)})
+        return remote(tok_hbm, arrived.at[slots[k]], a_send, a_recv, slots[k], {"ep": peers[k]})
+
+    def forward_copy():
+        return remote(arrived.at[slots[2]], arrived.at[2], a_send, a_recv, 2, {"ep": peers[1]})
 
     def core_copy(k):
         return remote(part.at[k, other], from_core.at[k], core_send, core_recv, k, sibling)
@@ -62,10 +85,46 @@
         return remote(hidden.at[k, core], hidden.at[k, core], hid_send, hid_recv, k, sibling)
 
     def c_copy(k):
-        return remote(result.at[k], returned.at[k], c_send, c_recv, k, {"ep": partner(e, k)})
-
-    for k in range(1, N):
-        a_copy(k).start()
+        return remote(result.at[k], returned.at[slots[k]], c_send, c_recv, slots[k], {"ep": peers[k]})
+
+    a_copy(1).start()
+
+    @pl.when(middle == 1)
+    def _():
+        a_copy(2).start()
+        for k in (1, 2):
+            pl.semaphore_signal(far_sem.at[0], inc=1, device_id={"ep": peers[k]}, device_id_type=MESH)
+
+    def second_sends():
+        a_copy(1).wait_send()
+        pl.semaphore_wait(far_sem.at[0], 1)
+
+        @pl.when(middle == 1)
+        def _():
+            pl.semaphore_signal(far_sem.at[1], inc=1, device_id={"ep": peers[1]}, device_id_type=MESH)
+
+        @pl.when(middle == 0)
+        def _():
+            a_copy(2).start()
+
+    def forward():
+        @pl.when(middle == 1)
+        def _():
+            a_copy(2).wait_recv()
+            forward_copy().start()
+
+    def third_send(after):
+        @pl.when(middle == 0)
+        def _():
+            if after:
+                a_copy(2).wait_send()
+            pl.semaphore_wait(far_sem.at[1], 1)
+            a_copy(3).start()
+
+        if after:
+            @pl.when(middle == 1)
+            def _():
+                a_copy(2).wait_send()
 
     half = rows // 2
 
@@ -76,16 +135,20 @@
     diagonal = lax.broadcasted_iota(jnp.int32, square, 0) == lax.broadcasted_iota(jnp.int32, square, 1)
     factors = []
     for k in range(N):
-        row = jnp.sum(jnp.where(routes == partner(e, k), weights, 0.0), axis=0, keepdims=True)
+        row = jnp.sum(jnp.where(routes == peers[k], weights, 0.0), axis=0, keepdims=True)
         factors.append(jnp.sum(jnp.where(diagonal, row, 0.0), axis=1, keepdims=True))
 
     def up_stage(k):
         if k == 0:
             load_tok.wait()
             load_up.wait()
+        elif k == 2:
+            @pl.when(middle == 0)
+            def _():
+                a_copy(2).wait_recv()
         else:
             a_copy(k).wait_recv()
-        value = jnp.dot(arrived[k], up[...], preferred_element_type=jnp.float32).astype(jnp.bfloat16)
+        value = jnp.dot(arrived[slots[k]], up[...], preferred_element_type=jnp.float32).astype(jnp.bfloat16)
         part[k] = value.reshape(2, half, value.shape[1])
         core_copy(k).start()
 
@@ -114,17 +177,22 @@
             result[k] = value
             c_copy(k).start()
 
-    order = (0, 1, 3, 2)
-    for t in range(N + 3):
-        for lag, stage in ((3, down_stage), (2, hidden_stage), (1, chip_stage), (0, up_stage)):
-            if 0 <= t - lag < N:
-                stage(order[t - lag])
+    stages = {"u": up_stage, "c": chip_stage, "h": hidden_stage, "d": down_stage}
+    for step in SCHEDULE.split():
+        if step == "S2":
+            second_sends()
+        elif step == "F":
+            forward()
+        elif step in ("S3", "X3"):
+            third_send(step == "S3")
+        else:
+            stages[step[0]](int(step[1]))
 
     mixed = jnp.zeros(out_ref.shape, jnp.float32)
-    for k in order:
+    for k in range(N):
         if k > 0:
             c_copy(k).wait_recv()
-        mixed = mixed + factors[k] * returned[k].astype(jnp.float32)
+        mixed = mixed + factors[k] * returned[slots[k]].astype(jnp.float32)
     out_ref[...] = mixed.astype(out_ref.dtype)
 
     for k in range(N):
@@ -132,7 +200,8 @@
         chip_copy(k).wait_send()
         hid_copy(k).wait_send()
         if k > 0:
-            a_copy(k).wait_send()
+            if k == 3 or (k == 2 and "X3" in SCHEDULE):
+                a_copy(k).wait_send()
             c_copy(k).wait_send()
 
 
@@ -162,7 +231,7 @@
             pltpu.VMEM((N, rows, quarter), bf16),
             pltpu.VMEM((N, rows, quarter), bf16),
             dma((3,)),
-        ] + [dma((N,))] * 10,
+        ] + [dma((N,))] * 10 + [pltpu.SemaphoreType.REGULAR((2,))],
         compiler_params=pltpu.CompilerParams(
             collective_id=0, has_side_effects=True, vmem_limit_bytes=60 * 1024 * 1024
         ),

time: 38.3 us -> 33.6 us (0.88)
  Pallas kernels: 36.5 us -> 31.8 us
    pallas_call x1, Pallas kernels: 36.5 us -> 31.8 us  [dense_body(): pl.pallas_call(kernel, out_shape=jax.ShapeDtypeStruct((rows, quarter), bf...]
where the time goes in v2:
time: 33.6 us; the launch traced here: 33.4 us
  Pallas kernels  31.8 us (95%)
  local copies, waits for them, and re-layouts  1.55 us (5%)
    pallas_call x1, Pallas kernels, dense_body(): pl.pallas_call(kernel, out_shape=jax.ShapeDtypeStruct((rows, quarter), bf...  31.8 us
    unnamed x1, local copies, waits for them, and re-layouts  1.55 us

profile of v2, /device:TPU:0, one launch (start us, length us, event | category | flops | bytes accessed | tf_op | source)
XLA Modules:
  0.0 33.4 jit_solution(13980239678926855963)
XLA Ops:
  0.0 31.8 %expert_layer.1 = bf16[64,896]{1,0:T(8,128)(2,1)} custom-call(bf16[64,896]{1,0:T(8,128)(2,1)} %tok_hbm.1, s32[2,64]{1,0:T(2,128)} %bitcast.2, f32[2,64]{1,0:T(2,128)} %bitcast.3, bf16[1,896,1024]{2,1,0:T(8,128)(2,1)} %up_hbm.1, bf16[1,1024,896]{2,1,0:T(8,128)(2,1)} %down_hbm.1), custom_call_target="tpu_custom_call" | custom-call | flops 939524096 | bytes 3670016 | tf_op jit(solution)/shard_map/expert_layer/pallas_call | solution.py:216
  31.8 1.6 %copy.7 = bf16[64,896]{1,0:T(8,128)(2,1)} copy(bf16[64,896]{1,0:T(8,128)(2,1)} %expert_layer.1) | data formatting | bytes 229376

commit v3 on v2

--- a/solution.py
+++ b/solution.py
@@ -13,22 +13,20 @@
 
 
 SCHEDULE = (
-    "u0 c0 S2 u1 "
-    "F c1 S3 h0 "
-    "d0 u2 c2 u3 "
-    "c3 h1 d1 h2 "
-    "d2 h3 d3 "
+    "u0", "S2", "c0", "u1", "c1", "X3", "h0", "u2", "c2", "h1",
+    "u3", "c3", "d1", "h2", "d2", "h3", "d3", "d0",
 )
 
 
 def partners(e):
     middle = lax.rem((e + 1) // 2, 2)
-    slots = (0, 1, 2 + middle, 3 - middle)
+    slots = (0, 1 + 2 * middle, 2 - middle, 3 - middle)
     near = e + 1 - 2 * lax.rem(e, 2)
     cross, flip = lax.rem(e + 2, N), N - 1 - e
-    second = middle * flip + (1 - middle) * cross
+    first = middle * flip + (1 - middle) * near
+    second = middle * near + (1 - middle) * cross
     third = middle * cross + (1 - middle) * flip
-    return middle, slots, (e, near, second, third)
+    return middle, slots, (e, first, second, third)
 
 
 def kernel(
@@ -73,7 +71,7 @@
         return remote(tok_hbm, arrived.at[slots[k]], a_send, a_recv, slots[k], {"ep": peers[k]})
 
     def forward_copy():
-        return remote(arrived.at[slots[2]], arrived.at[2], a_send, a_recv, 2, {"ep": peers[1]})
+        return remote(arrived.at[slots[1]], arrived.at[2], a_send, a_recv, 2, {"ep": peers[2]})
 
     def core_copy(k):
         return remote(part.at[k, other], from_core.at[k], core_send, core_recv, k, sibling)
@@ -101,17 +99,11 @@
 
         @pl.when(middle == 1)
         def _():
-            pl.semaphore_signal(far_sem.at[1], inc=1, device_id={"ep": peers[1]}, device_id_type=MESH)
+            pl.semaphore_signal(far_sem.at[1], inc=1, device_id={"ep": peers[2]}, device_id_type=MESH)
 
         @pl.when(middle == 0)
         def _():
             a_copy(2).start()
-
-    def forward():
-        @pl.when(middle == 1)
-        def _():
-            a_copy(2).wait_recv()
-            forward_copy().start()
 
     def third_send(after):
         @pl.when(middle == 0)
@@ -142,12 +134,13 @@
         if k == 0:
             load_tok.wait()
             load_up.wait()
-        elif k == 2:
-            @pl.when(middle == 0)
-            def _():
-                a_copy(2).wait_recv()
         else:
             a_copy(k).wait_recv()
+        if k == 1:
+            @pl.when(middle == 1)
+            def _():
+                forward_copy().start()
+
         value = jnp.dot(arrived[slots[k]], up[...], preferred_element_type=jnp.float32).astype(jnp.bfloat16)
         part[k] = value.reshape(2, half, value.shape[1])
         core_copy(k).start()
@@ -167,7 +160,7 @@
 
     def down_stage(k):
         hid_copy(k).wait_recv()
-        if k == 0:
+        if k == 1:
             load_down.wait()
         rows_in = hidden[k].reshape(rows, hidden.shape[3])
         value = jnp.dot(rows_in, down[...], preferred_element_type=jnp.float32).astype(jnp.bfloat16)
@@ -178,11 +171,9 @@
             c_copy(k).start()
 
     stages = {"u": up_stage, "c": chip_stage, "h": hidden_stage, "d": down_stage}
-    for step in SCHEDULE.split():
+    for step in SCHEDULE:
         if step == "S2":
             second_sends()
-        elif step == "F":
-            forward()
         elif step in ("S3", "X3"):
             third_send(step == "S3")
         else:

time: 33.6 us -> 32.6 us (0.970)
  Pallas kernels: 31.8 us -> 30.9 us
    pallas_call x1, Pallas kernels: 31.8 us -> 30.9 us  [dense_body(): pl.pallas_call(kernel, out_shape=jax.ShapeDtypeStruct((rows, quarter), bf...]
where the time goes in v3:
time: 32.6 us; the launch traced here: 32.4 us
  Pallas kernels  30.9 us (95%)
  local copies, waits for them, and re-layouts  1.55 us (5%)
    pallas_call x1, Pallas kernels, dense_body(): pl.pallas_call(kernel, out_shape=jax.ShapeDtypeStruct((rows, quarter), bf...  30.9 us
    unnamed x1, local copies, waits for them, and re-layouts  1.55 us

profile of v3, /device:TPU:0, one launch (start us, length us, event | category | flops | bytes accessed | tf_op | source)
XLA Modules:
  0.0 32.4 jit_solution(1875532986587809303)
XLA Ops:
  0.0 30.9 %expert_layer.1 = bf16[64,896]{1,0:T(8,128)(2,1)} custom-call(bf16[64,896]{1,0:T(8,128)(2,1)} %tok_hbm.1, s32[2,64]{1,0:T(2,128)} %bitcast.2, f32[2,64]{1,0:T(2,128)} %bitcast.3, bf16[1,896,1024]{2,1,0:T(8,128)(2,1)} %up_hbm.1, bf16[1,1024,896]{2,1,0:T(8,128)(2,1)} %down_hbm.1), custom_call_target="tpu_custom_call" | custom-call | flops 939524096 | bytes 3670016 | tf_op jit(solution)/shard_map/expert_layer/pallas_call | solution.py:207
  30.9 1.6 %copy.7 = bf16[64,896]{1,0:T(8,128)(2,1)} copy(bf16[64,896]{1,0:T(8,128)(2,1)} %expert_layer.1) | data formatting | bytes 229376
